TPU v7x, 256 devices: a whole 4x4x8 slice. The times are simulated.
256 devices in a mesh: row: 8 (over x_hi, y), col: 16 (over z, core), dp: 2 (over x_lo).
Axes of the slice: x: 4 (x_hi: 2, x_lo: 2; x = x_hi * 2 + x_lo), y: 4, z: 8, core: 2. Of those that a mesh axis runs over, the one named last changes fastest.
Arguments:
- tokens: bfloat16 [1536, 5120], P(('col', 'dp'), 'row'), may hold values from -6 to 6
- w_gate: bfloat16 [5120, 14336], P('row', 'col'), may hold values from -0.078125 to 0.078125
- w_up: bfloat16 [5120, 14336], P('row', 'col'), may hold values from -0.078125 to 0.078125
- w_down: bfloat16 [14336, 5120], P('col', 'row'), may hold values from -0.046875 to 0.046875
- grad_out: bfloat16 [1536, 5120], P(('col', 'dp'), 'row'), may hold values from -6 to 6
Outputs:
- mixed: bfloat16 [1536, 5120], P(('col', 'dp'), 'row')
- grad_tokens: bfloat16 [1536, 5120], P(('col', 'dp'), 'row')
- grad_w_gate: bfloat16 [5120, 14336], P(('row', 'dp'), 'col')
- grad_w_up: bfloat16 [5120, 14336], P(('row', 'dp'), 'col')
- grad_w_down: bfloat16 [14336, 5120], P('col', ('row', 'dp'))
All inputs are finite; a program needn't handle non-finite values.
Results may differ from a plain program's by a relative error of at most 0.005.
Values may be sent and summed in bfloat16 or wider, within the bound.
A program may use at most 128 MiB of HBM per device.

v0:
```python
import jax
import jax.numpy as jnp
from jax import lax
from jax.sharding import PartitionSpec as P


def contract_last(left, right):
    return lax.dot_general(
        left, right, (((1,), (1,)), ((), ())), preferred_element_type=jnp.float32
    )


def contract_first(left, right):
    return lax.dot_general(
        left, right, (((0,), (0,)), ((), ())), preferred_element_type=jnp.float32
    )


def per_device(tokens, w_gate, w_up, w_down, grad_out):
    width_cols = w_gate.shape[1]
    stacked = jnp.concatenate([w_gate, w_up], axis=1)
    rows_all = lax.all_gather(tokens, "col", axis=0, tiled=True)
    piece = rows_all
    pre = lax.psum_scatter(
        jnp.dot(piece, stacked, preferred_element_type=jnp.float32),
        "row",
        scatter_dimension=0,
        tiled=True,
    )
    gate = pre[:, :width_cols]
    up = pre[:, width_cols:]
    sig = jax.nn.sigmoid(gate)
    hidden = (gate * sig * up).astype(jnp.bfloat16)
    hidden_all = lax.all_gather(hidden, "row", axis=0, tiled=True)
    piece = hidden_all
    mixed = lax.psum_scatter(
        jnp.dot(piece, w_down, preferred_element_type=jnp.float32),
        "col",
        scatter_dimension=0,
        tiled=True,
    ).astype(jnp.bfloat16)
    grad_all = lax.all_gather(grad_out, "col", axis=0, tiled=True)
    piece = grad_all
    grad_hidden = lax.psum_scatter(
        contract_last(piece, w_down), "row", scatter_dimension=0, tiled=True
    )
    grad_up = (grad_hidden * gate * sig).astype(jnp.bfloat16)
    grad_gate = (grad_hidden * up * sig * (1.0 + gate * (1.0 - sig))).astype(jnp.bfloat16)
    pre_grad = jnp.concatenate([grad_gate, grad_up], axis=1)
    pre_grad_all = lax.all_gather(pre_grad, "row", axis=0, tiled=True)
    piece = pre_grad_all
    grad_tokens = lax.psum_scatter(
        contract_last(piece, stacked), "col", scatter_dimension=0, tiled=True
    ).astype(jnp.bfloat16)
    stacked_grad = contract_first(rows_all, pre_grad_all)
    down_grad = contract_first(hidden_all, grad_all)
    stacked_sum, down_sum = (
        lax.psum_scatter(stacked_grad, "dp", scatter_dimension=0, tiled=True),
        lax.psum_scatter(down_grad, "dp", scatter_dimension=1, tiled=True),
    )
    grad_w_gate = stacked_sum[:, :width_cols].astype(jnp.bfloat16)
    grad_w_up = stacked_sum[:, width_cols:].astype(jnp.bfloat16)
    grad_w_down = down_sum.astype(jnp.bfloat16)
    return (mixed, grad_tokens, grad_w_gate, grad_w_up, grad_w_down)


def solution(mesh):
    placed = (
        P(("col", "dp"), "row"),
        P("row", "col"),
        P("row", "col"),
        P("col", "row"),
        P(("col", "dp"), "row"),
    )
    return jax.shard_map(
        per_device,
        mesh=mesh,
        in_specs=placed,
        out_specs=(
            P(("col", "dp"), "row"),
            P(("col", "dp"), "row"),
            P(("row", "dp"), "col"),
            P(("row", "dp"), "col"),
            P("col", ("row", "dp")),
        ),
        check_vma=False,
    )
```

profile of v0, /device:TPU:4, one launch (start us, length us, event | category | flops | bytes accessed | tf_op | source)
XLA Modules:
  0.0 578.5 jit_solution(17222606858451525740)
XLA Ops:
  7.2 0.0 copy-start
  7.2 0.0 reduce-scatter.21.cloned.1.call-start
  7.2 23.1 %all_gather.14 = bf16[768,640]{1,0:T(8,128)(2,1)S(1)} all-gather(bf16[48,640]{1,0:T(8,128)(2,1)} %param.9), channel_id=1, replica_groups=mesh['row'=8,'col'=16,'dp'=2] {'col'}, dimensions={0}, use_global_device_ids=true | all-gather | bytes 1044480 | tf_op jit(solution)/shard_map/all_gather | solution.py:42
  30.3 0.9 copy-done.5
  31.3 0.0 copy-done
  31.3 3.0 fusion.3
  34.3 0.0 reduce-scatter.21.cloned.1.call-update
  34.3 0.0 copy-start.8
  34.3 0.0 reduce-scatter.19.cloned.1.call-start
  34.4 1.2 copy-done.1
  35.5 0.1 constant_dynamic-update-slice_fusion.1
  35.6 0.2 copy-done.2
  35.9 0.2 constant_dynamic-update-slice_fusion
  36.1 0.0 copy-done.8
  36.1 0.0 copy-start.7
  36.1 17.3 %all_gather.12 = bf16[768,640]{1,0:T(8,128)(2,1)S(1)} all-gather(bf16[48,640]{1,0:T(8,128)(2,1)S(1)} %copy-done.8), channel_id=1, replica_groups=mesh['row'=8,'col'=16,'dp'=2] {'col'}, dimensions={0}, use_global_device_ids=true | all-gather | bytes 1044480 | tf_op jit(solution)/shard_map/all_gather | solution.py:22
  53.4 0.0 copy-done.7
  53.4 1.0 copy-done.3
  54.4 4.9 convolution_bitcast_fusion
  59.2 6.2 %copy.19 = f32[768,1792]{1,0:T(8,128)} copy(f32[768,1792]{0,1:T(8,128)} %convolution_bitcast_fusion) | data formatting | bytes 11010048
  65.4 0.0 reduce-scatter.19.cloned.1.call-update
  65.4 0.0 all-gather.3.cloned.1.call-start
  65.4 48.3 %reduce-scatter.21.cloned.1.call-done = f32[96,896]{1,0:T(8,128)} async-done(((f32[768,896]{1,0:T(8,128)}), f32[96,896]{1,0:T(8,128)}) %reduce-scatter.21.cloned.1.call-update) | async-done | bytes 344080
  113.8 1.2 copy.22
  115.0 99.4 %reduce-scatter.19.cloned.1.call-done = f32[96,1792]{1,0:T(8,128)} async-done(((f32[768,1792]{1,0:T(8,128)}), f32[96,1792]{1,0:T(8,128)}) %reduce-scatter.19.cloned.1.call-update) | async-done | bytes 688144
  214.4 1.1 fusion.1
  215.5 0.2 copy.25
  215.7 0.2 copy.26
  215.9 0.3 multiply_convert_fusion.1
  216.2 0.8 copy.13
  217.0 0.0 all-gather.3.cloned.1.call-update
  217.0 0.0 all-gather.5.cloned.1.call-start
  217.1 0.1 pad_maximum_fusion
  217.2 0.9 copy.15
  218.1 0.0 all-gather.5.cloned.1.call-update
  218.1 0.0 copy-start.6
  218.2 0.0 reduce-scatter.13.cloned.1.call-start
  218.2 51.8 %all-gather.3.cloned.1.call-done = bf16[768,896]{1,0:T(8,128)(2,1)} async-done(((bf16[96,896]{1,0:T(8,128)(2,1)}), bf16[768,896]{1,0:T(8,128)(2,1)}) %all-gather.3.cloned.1.call-update) | async-done | bytes 1376272 | tf_op jit(solution)/shard_map/all_gather | solution.py:34
  270.0 4.2 fusion.2
  274.2 0.0 reduce-scatter.13.cloned.1.call-update
  274.2 0.0 reduce-scatter.17.cloned.1.call-start
  274.2 0.0 copy-done.6
  274.3 0.0 copy-done.9
  274.3 2.6 fusion.5
  276.9 0.0 reduce-scatter.17.cloned.1.call-update
  276.9 0.0 reduce-scatter.15.cloned.1.call-start
  277.0 59.9 %all-gather.5.cloned.1.call-done = bf16[768,1792]{1,0:T(8,128)(2,1)} async-done(((bf16[96,1792]{1,0:T(8,128)(2,1)}), bf16[768,1792]{1,0:T(8,128)(2,1)}) %all-gather.5.cloned.1.call-update) | async-done | bytes 2752528 | tf_op jit(solution)/shard_map/all_gather | solution.py:50
  336.8 6.1 %fusion.4 = f32[768,640]{1,0:T(8,128)} fusion(bf16[768,1792]{1,0:T(8,128)(2,1)} %all-gather.5.cloned.1.call-done, bf16[640,1792]{1,0:T(8,128)(2,1)} %copy-done.7), kind=kOutput, calls=%fused_computation.13 | convolution fusion | flops 1761607680 | bytes 7012352 | tf_op jit(solution)/shard_map/dot_general | solution.py:8
  342.9 0.0 reduce-scatter.15.cloned.1.call-update
  342.9 0.2 reduce-scatter.23.cloned.1.call-start
  343.2 6.3 %convolution_bitcast_fusion.1 = f32[640,1792]{0,1:T(8,128)} fusion(bf16[768,1792]{1,0:T(8,128)(2,1)} %all-gather.5.cloned.1.call-done, bf16[768,640]{1,0:T(8,128)(2,1)S(1)} %copy-done.4), kind=kOutput, calls=%fused_computation.1 | convolution fusion | flops 1761607680 | bytes 8323072 | tf_op jit(solution)/shard_map/dot_general | solution.py:14
  349.4 5.7 copy.23
  355.1 0.0 reduce-scatter.23.cloned.1.call-update
  355.1 43.6 %reduce-scatter.13.cloned.1.call-done = f32[48,640]{1,0:T(8,128)} async-done(((f32[768,640]{1,0:T(8,128)}), f32[48,640]{1,0:T(8,128)}) %reduce-scatter.13.cloned.1.call-update) | async-done | bytes 122896 | tf_op jit(solution)/shard_map/reduce_scatter | solution.py:36
  398.7 1.5 convert_element_type.21
  400.3 37.9 %reduce-scatter.17.cloned.1.call-done = f32[896,320]{0,1:T(8,128)} async-done(((f32[896,640]{0,1:T(8,128)}), f32[896,320]{0,1:T(8,128)}) %reduce-scatter.17.cloned.1.call-update) | async-done | bytes 1146896 | tf_op jit(solution)/shard_map/reduce_scatter | solution.py:59
  438.2 2.1 convert_element_type.25
  440.3 60.9 %reduce-scatter.15.cloned.1.call-done = f32[48,640]{1,0:T(8,128)} async-done(((f32[768,640]{1,0:T(8,128)}), f32[48,640]{1,0:T(8,128)}) %reduce-scatter.15.cloned.1.call-update) | async-done | bytes 122896 | tf_op jit(solution)/shard_map/reduce_scatter | solution.py:52
  501.2 1.5 convert_element_type.24
  502.7 62.7 %reduce-scatter.23.cloned.1.call-done = f32[320,1792]{1,0:T(8,128)} async-done(((f32[640,1792]{1,0:T(8,128)}), f32[320,1792]{1,0:T(8,128)}) %reduce-scatter.23.cloned.1.call-update) | async-done | bytes 2293776
  565.4 2.0 copy.24
  567.4 1.0 fusion
  568.4 2.2 copy.16
  570.6 1.1 copy.17
  (7 shorter events, 0.0 us)
Async XLA Ops:
  7.2 24.1 %copy-start = (bf16[896,640]{1,0:T(8,128)(2,1)S(1)}, bf16[896,640]{1,0:T(8,128)(2,1)}, u32[]{:S(2)}) copy-start(bf16[896,640]{1,0:T(8,128)(2,1)} %param.8) | copy-start | bytes 3440644
  7.2 106.6 %reduce-scatter.21.cloned.1.call-start = ((), (), s32[]{:S(2)}) async-start(), calls=%async_computation.12 | async-start | bytes 3096576
  30.3 0.9 copy-start.5
  34.3 1.3 copy-start.1
  34.3 1.6 copy-start.2
  34.3 1.8 copy-start.8
  34.3 180.0 %reduce-scatter.19.cloned.1.call-start = ((), (), s32[]{:S(2)}) async-start(), calls=%async_computation.11 | async-start | bytes 6193152
  36.1 17.3 %copy-start.7 = (bf16[640,1792]{1,0:T(8,128)(2,1)}, bf16[640,1792]{1,0:T(8,128)(2,1)S(1)}, u32[]{:S(2)}) copy-start(bf16[640,1792]{1,0:T(8,128)(2,1)S(1)} %constant_dynamic-update-slice_fusion) | copy-start | bytes 6881284
  53.4 1.0 copy-start.3
  65.4 204.6 %all-gather.3.cloned.1.call-start = ((), (), s32[]{:S(2)}) async-start(), calls=%async_computation.6 | async-start | bytes 1548288 | tf_op jit(solution)/shard_map/all_gather | solution.py:34
  217.0 119.8 %all-gather.5.cloned.1.call-start = ((), (), s32[]{:S(2)}) async-start(), calls=%async_computation.8 | async-start | bytes 3096576 | tf_op jit(solution)/shard_map/all_gather | solution.py:50
  218.1 56.1 %copy-start.6 = (bf16[768,640]{1,0:T(8,128)(2,1)S(1)}, bf16[768,640]{1,0:T(8,128)(2,1)}, u32[]{:S(2)}) copy-start(bf16[768,640]{1,0:T(8,128)(2,1)} %copy-done.5) | copy-start | bytes 2949124
  218.2 180.6 %reduce-scatter.13.cloned.1.call-start = ((), (), s32[]{:S(2)}) async-start(), calls=%async_computation.7 | async-start | bytes 2088960 | tf_op jit(solution)/shard_map/reduce_scatter | solution.py:36
  270.0 4.3 copy-start.9
  274.2 164.0 %reduce-scatter.17.cloned.1.call-start = ((), (), s32[]{:S(2)}) async-start(), calls=%async_computation.10 | async-start | bytes 3440640 | tf_op jit(solution)/shard_map/reduce_scatter | solution.py:59
  276.9 66.3 %copy-start.4 = (bf16[768,640]{1,0:T(8,128)(2,1)S(1)}, bf16[768,640]{1,0:T(8,128)(2,1)}, u32[]{:S(2)}) copy-start(bf16[768,640]{1,0:T(8,128)(2,1)} %copy-done.3) | copy-start | bytes 2949124
  276.9 224.3 %reduce-scatter.15.cloned.1.call-start = ((), (), s32[]{:S(2)}) async-start(), calls=%async_computation.9 | async-start | bytes 2088960 | tf_op jit(solution)/shard_map/reduce_scatter | solution.py:52
  342.9 222.5 %reduce-scatter.23.cloned.1.call-start = ((), (), s32[]{:S(2)}) async-start(), calls=%async_computation.13 | async-start | bytes 6881280
Sparse Core Ops, SparseCore 0:
  34.4 79.3 reduce-scatter.20
  117.9 96.3 reduce-scatter.18
  217.9 52.0 all-gather.2
  273.4 63.4 all-gather.4
  339.4 59.3 reduce-scatter.12
  401.1 37.0 reduce-scatter.16
  440.9 60.2 reduce-scatter.14
  503.8 61.6 reduce-scatter.22
where the time goes:
time: 580 us; the launch traced here: 579 us
  waiting for transfers between devices  465 us (80%)
  blocking collectives  40.4 us (7%)
  matrix products  27 us (5%)
  local copies, waits for them, and re-layouts  26.2 us (5%)
  between operations  14.3 us (2%)
    unnamed x11, waiting for transfers between devices  211 us
    reduce_scatter x1, waiting for transfers between devices, per_device(): lax.psum_scatter(contract_last(piece, stacked), 'col', scatter_dimension=...  60.9 us
    all_gather x1, waiting for transfers between devices, per_device(): pre_grad_all = lax.all_gather(pre_grad, 'row', axis=0, tiled=True)  59.9 us
    all_gather x1, waiting for transfers between devices, per_device(): hidden_all = lax.all_gather(hidden, 'row', axis=0, tiled=True)  51.8 us
    reduce_scatter x1, waiting for transfers between devices, per_device(): lax.psum_scatter(jnp.dot(piece, w_down, preferred_element_type=jnp.float3...  43.6 us
    reduce_scatter x1, waiting for transfers between devices, per_device(): lax.psum_scatter(down_grad, 'dp', scatter_dimension=1, tiled=True)  37.9 us
    all_gather x1, blocking collectives, per_device(): grad_all = lax.all_gather(grad_out, 'col', axis=0, tiled=True)  23.1 us
    unnamed x29, local copies, waits for them, and re-layouts  22.1 us
  transfers between devices with their start and end apart: 8, of which 8 were waited for; matrix products, arithmetic and copies ran while one was open for 8% of the time, Pallas kernels for 0%

commit v1 on v0

v1 whole, which is shorter than its diff:
```python
import functools

import jax
import jax.numpy as jnp
from jax import lax
from jax.experimental import pallas as pl
from jax.experimental.pallas import tpu as pltpu
from jax.sharding import PartitionSpec as P

MESH = pl.DeviceIdType.MESH
BF16, F32 = jnp.bfloat16, jnp.float32
NY, NZ = 4, 8
CUT = 512


def dot(a, b):
    return jnp.dot(a, b, preferred_element_type=F32)


def dot_last(a, b):
    return lax.dot_general(a, b, (((1,), (1,)), ((), ())), preferred_element_type=F32)


def dot_first(a, b):
    return lax.dot_general(a, b, (((0,), (0,)), ((), ())), preferred_element_type=F32)


def flat(x):
    return x.reshape((-1, x.shape[-1]))


class Links:
    def __init__(self, send, recv):
        self.send, self.recv = send, recv
        self.n_send = self.n_recv = 0
        self.started = []

    def slots(self, n=1):
        first = self.n_recv
        self.n_recv += n
        return first

    def copy(self, src, dst, slot, to):
        c = pltpu.make_async_remote_copy(
            src_ref=src,
            dst_ref=dst,
            send_sem=self.send.at[self.n_send],
            recv_sem=self.recv.at[slot],
            device_id=to,
            device_id_type=MESH,
        )
        self.n_send += 1
        return c

    def put(self, src, dst, slot, to):
        c = self.copy(src, dst, slot, to)
        c.start()
        self.started.append((c, None))

    def put_or_keep(self, src, dst, slot, to, away):
        c = self.copy(src, dst, slot, to)

        @pl.when(away == 1)
        def _():
            c.start()

        @pl.when(away == 0)
        def _():
            pltpu.make_async_copy(src, dst, self.recv.at[slot]).start()

        self.started.append((c, away))

    def arrived(self, dst, slot):
        pltpu.make_async_copy(dst, dst, self.recv.at[slot]).wait()

    def finish(self):
        for c, away in self.started:
            if away is None:
                c.wait_send()
            else:
                pl.when(away == 1)(c.wait_send)


def kernel(
    tok, wg_h, wu_h, wd_h, go, mixed_o, gt_o, gwg_o, gwu_o, gwd_o,
    tok_a, go_a, wg, wu, wd, tok_t,
    g_p, g_f, g_x, g_s, g_y, u_p, u_f, u_y, u_s, u_x,
    h1_p, h1_f, h1_x, h1_s, h1_y, h2_p, h2_f, h2_y, h2_s, h2_x,
    gate_v, up_v, sig_v, hid_a, gg_a, gu_a,
    part1, part2, pair1, pair2, zs1, zs2, zr1, zr2,
    dw_f, dw_s, dw_r, gw_f, gw_s, gw_r,
    send, recv, loc,
):
    row, col, l = lax.axis_index("row"), lax.axis_index("col"), lax.axis_index("dp")
    h, y = row // NY, lax.rem(row, NY)
    z, k = col // 2, lax.rem(col, 2)
    l1 = l + h - 2 * l * h

    def dev(hh, yy, zz, kk, ll):
        return (hh * NY + yy, zz * 2 + kk, ll)

    def ys(d):
        return lax.rem(y + d, NY)

    def zs(d):
        return lax.rem(z + d + NZ, NZ)

    over_y = [None] + [dev(h, ys(d), z, k, l) for d in (1, 2, 3)]
    over_x = dev(1 - h, y, z, k, 1 - l)
    twin = (row, col, 1 - l)
    core = dev(h, y, z, 1 - k, l)

    loads = []
    for i, (src, dst) in enumerate(((wg_h, wg), (wu_h, wu), (wd_h, wd))):
        c = pltpu.make_async_copy(src, dst, loc.at[i])
        c.start()
        loads.append(c)

    barrier = pltpu.get_barrier_semaphore()
    friends = [over_x, twin, core, dev(h, y, z, 1 - k, 1 - l)] + over_y[1:]
    for d in range(1, NZ):
        for ll in (l, 1 - l):
            friends.append(dev(h, y, zs(d), k, ll))
    for to in friends:
        pl.semaphore_signal(barrier, inc=1, device_id=to, device_id_type=MESH)
    pl.semaphore_wait(barrier, len(friends))

    net = Links(send, recv)

    side = 1 - 2 * k
    gathers = [(src, dst, net.slots(16)) for src, dst in ((tok, tok_a), (go, go_a))]

    def gather_put(dst, base, origin, to):
        net.put(dst.at[origin], dst.at[origin], base + origin, to)

    for src, dst, base in gathers:
        for to in (dev(h, y, zs(side), k, l1), dev(h, y, zs(-side), k, l1), dev(h, y, z, 1 - k, l1)):
            net.put(src, dst.at[col], base + col, to)
        net.put_or_keep(src, dst.at[col], base + col, dev(h, y, z, k, l1), h)
    for step in range(1, 5):
        for src, dst, base in gathers:
            far = zs(-side * step) * 2 + k
            net.arrived(dst.at[far], base + far)
            if step < 4:
                gather_put(dst, base, far, dev(h, y, zs(side), k, l))
            gather_put(dst, base, far, core)
            if step < 4:
                near = zs(side * step) * 2 + k
                net.arrived(dst.at[near], base + near)
                if step < 3:
                    gather_put(dst, base, near, dev(h, y, zs(-side), k, l))
                gather_put(dst, base, near, core)
    for src, dst, base in gathers:
        net.arrived(dst.at[col], base + col)
        for zz in range(NZ):
            other = zz * 2 + 1 - k
            net.arrived(dst.at[other], base + other)

    def rows_of(ref, half, q):
        return flat(ref[pl.ds(half * 8 + q * 4, 4)])

    def x_first_send(ref, mm, p, x):
        slot = net.slots(2)
        for q in range(2):
            out = mm(rows_of(ref, 1 - h, q))
            p[pl.ds(2 * q, 2)] = out.astype(BF16).reshape((2, 96, -1))
            net.put(p.at[pl.ds(2 * q, 2)], x.at[pl.ds(2 * q, 2)], slot + q, over_x)
        return slot

    def x_first_own(ref, mm, f):
        for q in range(2):
            f[pl.ds(2 * q, 2)] = mm(rows_of(ref, h, q)).reshape((2, 96, -1))

    def x_first_pass(f, x, s, yr, slot):
        for q in range(2):
            net.arrived(x.at[pl.ds(2 * q, 2)], slot + q)
        for i in range(4):
            s[i] = (f[i] + x[i].astype(F32)).astype(BF16)
        slot = net.slots(3)
        for d in (1, 3, 2):
            net.put(s.at[ys(d)], yr.at[d - 1], slot + d - 1, over_y[d])
        return slot

    def x_first_sum(f, x, yr, slot):
        total = f[y] + x[y].astype(F32)
        for d in (1, 3, 2):
            net.arrived(yr.at[d - 1], slot + d - 1)
            total = total + yr[d - 1].astype(F32)
        return total

    def y_first_send(ref, mm, p, f, yr):
        for half in range(2):
            for q in range(2):
                out = mm(rows_of(ref, half, q)).reshape((2, 96, -1))
                f[half, pl.ds(2 * q, 2)] = out
                p[half, pl.ds(2 * q, 2)] = out.astype(BF16)
        slot = net.slots(3)
        for d in (1, 3, 2):
            net.put(p.at[:, ys(d)], yr.at[d - 1], slot + d - 1, over_y[d])
        return slot

    def y_first_pass(f, yr, s, x, slot):
        for d in (1, 3, 2):
            net.arrived(yr.at[d - 1], slot + d - 1)
        total = f[1 - h, y]
        for d in (1, 3, 2):
            total = total + yr[d - 1, 1 - h].astype(F32)
        s[...] = total.astype(BF16)
        slot = net.slots()
        net.put(s, x, slot, over_x)
        return slot

    def y_first_sum(f, yr, x, slot):
        total = f[h, y]
        for d in (1, 3, 2):
            total = total + yr[d - 1, h].astype(F32)
        net.arrived(x, slot)
        return total + x[...].astype(F32)

    def mm_g(a):
        return dot(a, wg[...])

    def mm_u(a):
        return dot(a, wu[...])

    def mm_h1(a):
        return dot_last(a, wd[:CUT])

    def mm_h2(a):
        return dot_last(a, wd[CUT:])

    loads[0].wait()
    g1 = x_first_send(tok_a, mm_g, g_p, g_x)
    loads[1].wait()
    u1 = y_first_send(tok_a, mm_u, u_p, u_f, u_y)
    x_first_own(tok_a, mm_g, g_f)
    loads[2].wait()
    h11 = x_first_send(go_a, mm_h1, h1_p, h1_x)
    h21 = y_first_send(go_a, mm_h2, h2_p, h2_f, h2_y)
    x_first_own(go_a, mm_h1, h1_f)
    g2 = x_first_pass(g_f, g_x, g_s, g_y, g1)
    u2 = y_first_pass(u_f, u_y, u_s, u_x, u1)
    tok_t[...] = flat(tok_a[...]).T
    gate = x_first_sum(g_f, g_x, g_y, g2)
    up = y_first_sum(u_f, u_y, u_x, u2)
    sig = jax.nn.sigmoid(gate)
    gate_v[...] = gate
    up_v[...] = up
    sig_v[...] = sig
    hid_a[h, y] = (gate * sig * up).astype(BF16)

    def spread(buf, lo, hi):
        cols = pl.ds(lo, hi - lo)
        slot = net.slots(8)

        def at(hh, yy):
            return buf.at[hh, yy, :, cols]

        for to in (over_x, over_y[1], over_y[3], over_y[2]):
            net.put(at(h, y), at(h, y), slot + row, to)
        return at, slot

    def relay_y(piece):
        at, slot = piece
        net.arrived(at(1 - h, y), slot + (1 - h) * NY + y)
        for d in (1, 3, 2):
            net.put(at(1 - h, y), at(1 - h, y), slot + (1 - h) * NY + y, over_y[d])

    def relay_y_rest(piece):
        at, slot = piece
        for d in (1, 3, 2):
            for hh in (h, 1 - h):
                net.arrived(at(hh, ys(d)), slot + hh * NY + ys(d))

    def relay_x(piece):
        at, slot = piece
        for d in (1, 3, 2):
            net.arrived(at(h, ys(d)), slot + h * NY + ys(d))
            net.put(at(h, ys(d)), at(h, ys(d)), slot + h * NY + ys(d), over_x)

    def relay_x_rest(piece):
        at, slot = piece
        for d in range(4):
            net.arrived(at(1 - h, ys(d)), slot + (1 - h) * NY + ys(d))

    width = hid_a.shape[-1]
    hid0 = spread(hid_a, 0, CUT)
    hid1 = spread(hid_a, CUT, width)
    h12 = x_first_pass(h1_f, h1_x, h1_s, h1_y, h11)
    h22 = y_first_pass(h2_f, h2_y, h2_s, h2_x, h21)
    relay_y(hid1)
    relay_x(hid0)
    for at, total in (
        (pl.ds(0, CUT), x_first_sum(h1_f, h1_x, h1_y, h12)),
        (pl.ds(CUT, width - CUT), y_first_sum(h2_f, h2_y, h2_x, h22)),
    ):
        gate, up, sig = gate_v[:, at], up_v[:, at], sig_v[:, at]
        gu_a[h, y, :, at] = (total * gate * sig).astype(BF16)
        gg_a[h, y, :, at] = (total * up * sig * (1.0 + gate * (1.0 - sig))).astype(BF16)
    gg0 = spread(gg_a, 0, CUT)
    gu0 = spread(gu_a, 0, CUT)
    gg1 = spread(gg_a, CUT, width)
    gu1 = spread(gu_a, CUT, width)

    relay_x_rest(hid0)
    relay_y_rest(hid1)

    def down_grad(lo, hi):
        for j in range(lo, hi, 128):
            at = pl.ds(j, 128)
            both = dot_first(flat(flat_rows(hid_a, at)), flat(go_a[...]))
            first, second = both[:, :320], both[:, 320:]
            mine = jnp.where(l == 0, first, second)
            dw_f[at] = mine
            dw_s[at] = jnp.where(l == 0, second, first).astype(BF16)
        slot = net.slots()
        at = pl.ds(lo, hi - lo)
        net.put(dw_s.at[at], dw_r.at[at], slot, twin)
        return slot, at

    def flat_rows(buf, at):
        return buf[:, :, :, at].reshape((8, 96, -1))

    dw0 = down_grad(0, CUT)
    relay_y(gu0)
    relay_x(gg0)
    dw1 = down_grad(CUT, width)

    def pair_send(part, pair):
        slot = net.slots()
        net.put(part.at[:, 1 - k], pair, slot, core)
        return slot

    def pair_pass(part, pair, zsend, zrecv, slot):
        net.arrived(pair, slot)
        for zz in range(NZ):
            zsend[zz] = (part[zz, k] + pair[zz]).astype(BF16)
        slot = net.slots(NZ)
        for d in (4, 3, 5, 2, 6, 1, 7):
            net.put(zsend.at[zs(d)], zrecv.at[d], slot + d, dev(h, y, zs(d), k, l1))
        net.put_or_keep(zsend.at[z], zrecv.at[0], slot, dev(h, y, z, k, l1), h)
        return slot

    def z_sum(zrecv, slot):
        total = None
        for d in range(NZ):
            net.arrived(zrecv.at[d], slot + d)
            block = zrecv[d].astype(F32)
            total = block if total is None else total + block
        return total.astype(BF16)

    def rows4(buf, i):
        half, q = i // 2, i % 2
        return flat(buf[half, pl.ds(2 * q, 2)])

    for i in range(4):
        part1[pl.ds(2 * i, 2)] = dot(rows4(hid_a, i), wd[...]).reshape((2, 2, 48, -1))
    m1 = pair_send(part1, pair1)
    relay_y(gu1)
    relay_x(gg1)

    def weight_grad(buf, first, lo, hi):
        at = pl.ds(lo, hi - lo)
        to = pl.ds(first + lo, hi - lo)
        for mine in (False, True):
            base = (l if mine else 1 - l) * 320
            for q in range(2):
                left = tok_t[pl.ds(pl.multiple_of(base + q * 160, 32), 160)]
                out = dot(left, flat(buf[:, :, :, at].reshape((8, 96, -1))))
                if mine:
                    gw_f[pl.ds(q * 160, 160), to] = out
                else:
                    gw_s[pl.ds(q * 160, 160), to] = out.astype(BF16)
            if not mine:
                slot = net.slots()
                net.put(gw_s.at[:, to], gw_r.at[:, to], slot, twin)
        return slot, to

    relay_x_rest(gg0)
    wg0 = weight_grad(gg_a, 0, 0, CUT)
    relay_y_rest(gu0)
    wu0 = weight_grad(gu_a, width, 0, CUT)
    m2 = pair_pass(part1, pair1, zs1, zr1, m1)
    relay_x_rest(gg1)
    wg1 = weight_grad(gg_a, 0, CUT, width)
    relay_y_rest(gu1)
    wu1 = weight_grad(gu_a, width, CUT, width)
    for i in range(4):
        out = dot_last(rows4(gg_a, i), wg[...]) + dot_last(rows4(gu_a, i), wu[...])
        part2[pl.ds(2 * i, 2)] = out.reshape((2, 2, 48, -1))
    t1 = pair_send(part2, pair2)
    for slot, at in (dw0, dw1):
        net.arrived(dw_r.at[at], slot)
        gwd_o[at] = (dw_f[at] + dw_r[at].astype(F32)).astype(BF16)
    t2 = pair_pass(part2, pair2, zs2, zr2, t1)
    mixed_o[...] = z_sum(zr1, m2)
    for out, (slot, at), lo, hi in (
        (gwg_o, wg0, 0, CUT), (gwu_o, wu0, 0, CUT), (gwg_o, wg1, CUT, width), (gwu_o, wu1, CUT, width),
    ):
        net.arrived(gw_r.at[:, at], slot)
        out[:, pl.ds(lo, hi - lo)] = (gw_f[:, at] + gw_r[:, at].astype(F32)).astype(BF16)
    gt_o[...] = z_sum(zr2, t2)
    net.finish()


def per_device(tokens, w_gate, w_up, w_down, grad_out):
    n_tok, d = tokens.shape
    f = w_gate.shape[1]
    rest = f - CUT

    def x_first(w):
        return [
            pltpu.VMEM((4, 96, w), BF16),
            pltpu.VMEM((4, 96, w), F32),
            pltpu.VMEM((4, 96, w), BF16),
            pltpu.VMEM((4, 96, w), BF16),
            pltpu.VMEM((3, 96, w), BF16),
        ]

    def y_first(w):
        return [
            pltpu.VMEM((2, 4, 96, w), BF16),
            pltpu.VMEM((2, 4, 96, w), F32),
            pltpu.VMEM((3, 2, 96, w), BF16),
            pltpu.VMEM((96, w), BF16),
            pltpu.VMEM((96, w), BF16),
        ]

    scratch = [
        pltpu.VMEM((16, n_tok, d), BF16),
        pltpu.VMEM((16, n_tok, d), BF16),
        pltpu.VMEM(w_gate.shape, BF16),
        pltpu.VMEM(w_up.shape, BF16),
        pltpu.VMEM(w_down.shape, BF16),
        pltpu.VMEM((d, 16 * n_tok), BF16),
        *x_first(f),
        *y_first(f),
        *x_first(CUT),
        *y_first(rest),
        *[pltpu.VMEM((96, f), F32)] * 3,
        *[pltpu.VMEM((2, 4, 96, f), BF16)] * 3,
        *[pltpu.VMEM((8, 2, n_tok, d), F32)] * 2,
        *[pltpu.VMEM((8, n_tok, d), F32)] * 2,
        *[pltpu.VMEM((8, n_tok, d), BF16)] * 4,
        pltpu.VMEM((f, d // 2), F32),
        pltpu.VMEM((f, d // 2), BF16),
        pltpu.VMEM((f, d // 2), BF16),
        pltpu.VMEM((d // 2, 2 * f), F32),
        pltpu.VMEM((d // 2, 2 * f), BF16),
        pltpu.VMEM((d // 2, 2 * f), BF16),
        pltpu.SemaphoreType.DMA((160,)),
        pltpu.SemaphoreType.DMA((160,)),
        pltpu.SemaphoreType.DMA((3,)),
    ]
    vmem, hbm = pl.BlockSpec(memory_space=pltpu.VMEM), pl.BlockSpec(memory_space=pl.ANY)
    return pl.pallas_call(
        kernel,
        out_shape=(
            jax.ShapeDtypeStruct((n_tok, d), BF16),
            jax.ShapeDtypeStruct((n_tok, d), BF16),
            jax.ShapeDtypeStruct((d // 2, f), BF16),
            jax.ShapeDtypeStruct((d // 2, f), BF16),
            jax.ShapeDtypeStruct((f, d // 2), BF16),
        ),
        in_specs=[vmem, hbm, hbm, hbm, vmem],
        out_specs=(vmem,) * 5,
        scratch_shapes=scratch,
        compiler_params=pltpu.CompilerParams(
            collective_id=0, has_side_effects=True, vmem_limit_bytes=62 * 2**20
        ),
        name="swiglu",
    )(tokens, w_gate, w_up, w_down, grad_out)


def solution(mesh):
    placed = (
        P(("col", "dp"), "row"),
        P("row", "col"),
        P("row", "col"),
        P("col", "row"),
        P(("col", "dp"), "row"),
    )
    return jax.shard_map(
        per_device,
        mesh=mesh,
        in_specs=placed,
        out_specs=(
            P(("col", "dp"), "row"),
            P(("col", "dp"), "row"),
            P(("row", "dp"), "col"),
            P(("row", "dp"), "col"),
            P("col", ("row", "dp")),
        ),
        check_vma=False,
    )
```

time: 580 us -> 152 us (0.26)
  waiting for transfers between devices: 465 us -> 0 us
  Pallas kernels: 0 us -> 146 us
  blocking collectives: 40.4 us -> 0 us
  matrix products: 27 us -> 0 us
  local copies, waits for them, and re-layouts: 26.2 us -> 5.14 us
  between operations: 14.3 us -> 0.68 us
    unnamed x11 -> x0, waiting for transfers between devices: 211 us -> none
    pallas_call x0 -> x1, Pallas kernels: none -> 146 us  [per_device(): pl.pallas_call(kernel, out_shape=(jax.ShapeDtypeStruct((n_tok, d), BF16),...]
    reduce_scatter x3 -> x0, waiting for transfers between devices: 142 us -> none  [the longest x1 60.9 us: per_device(): lax.psum_scatter(contract_last(piece, stacked), 'col', scatter_dimension=...]
    all_gather x2 -> x0, waiting for transfers between devices: 112 us -> none  [the longest x1 59.9 us: per_device(): pre_grad_all = lax.all_gather(pre_grad, 'row', axis=0, tiled=True)]
    all_gather x2 -> x0, blocking collectives: 40.4 us -> none  [the longest x1 23.1 us: per_device(): grad_all = lax.all_gather(grad_out, 'col', axis=0, tiled=True)]
    dot_general x5 -> x0, matrix products: 24 us -> none  [the longest x2 8.86 us: contract_first(): lax.dot_general(left, right, (((0,), (0,)), ((), ())), preferred_element_...]
    unnamed x29 -> x12, local copies, waits for them, and re-layouts: 22.1 us -> 2.88 us
  transfers between devices with their start and end apart: 8 -> 0, of which waited for: 8 -> 0; matrix products, arithmetic and copies ran while one was open for 8% -> 0% of each run, Pallas kernels for 0% -> 0%
where the time goes in v1:
time: 152 us
  Pallas kernels  146 us (96%)
  local copies, waits for them, and re-layouts  5.14 us (3%)
    pallas_call x1, Pallas kernels, per_device(): pl.pallas_call(kernel, out_shape=(jax.ShapeDtypeStruct((n_tok, d), BF16),...  146 us

profile of v1, /device:TPU:4, one launch (start us, length us, event | category | flops | bytes accessed | tf_op | source)
XLA Modules:
  0.0 152.1 jit_solution(10563820666981708881)
XLA Ops:
  0.6 146.3 %swiglu.1 = (bf16[48,640]{1,0:T(8,128)(2,1)}, bf16[48,640]{1,0:T(8,128)(2,1)}, bf16[320,896]{1,0:T(8,128)(2,1)}, bf16[320,896]{1,0:T(8,128)(2,1)}, bf16[896,320]{1,0:T(8,128)(2,1)}) custom-call(bf16[48,640]{1,0:T(8,128)(2,1)} %tok.1, bf16[640,896]{1,0:T(8,128)(2,1)} %wg_h.1, bf16[640,896]{1,0:T(8,128)(2,1)} %wu_h.1, bf16[896,640]{1,0:T(8,128)(2,1)} %wd_h.1, ...), custom_call_target="tpu_custom_call" | custom-call | tf_op jit(solution)/shard_map/swiglu/pallas_call | solution.py:456
  146.9 0.0 copy-start.3
  146.9 0.0 copy-start.2
  147.0 0.0 copy-start.1
  147.0 0.0 copy-start
  147.0 2.3 %copy.10 = bf16[896,320]{0,1:T(8,128)(2,1)} copy(bf16[896,320]{1,0:T(8,128)(2,1)} %get-tuple-element.9) | data formatting | bytes 1146880 | tf_op jit(solution)/shard_map/swiglu/pallas_call | solution.py:456
  149.2 0.0 copy-done.3
  149.2 0.6 copy.15
  149.9 0.0 copy-done.2
  149.9 0.6 copy.16
  150.5 0.0 copy-done.1
  150.5 0.8 copy.17
  151.3 0.0 copy-done
  151.3 0.8 copy.18
Async XLA Ops:
  146.9 2.3 %copy-start.3 = (bf16[48,640]{1,0:T(8,128)(2,1)S(1)}, bf16[48,640]{1,0:T(8,128)(2,1)}, u32[]{:S(2)}) copy-start(bf16[48,640]{1,0:T(8,128)(2,1)} %get-tuple-element.15) | copy-start | bytes 184324
  146.9 2.9 %copy-start.2 = (bf16[48,640]{1,0:T(8,128)(2,1)S(1)}, bf16[48,640]{1,0:T(8,128)(2,1)}, u32[]{:S(2)}) copy-start(bf16[48,640]{1,0:T(8,128)(2,1)} %get-tuple-element.16) | copy-start | bytes 184324
  147.0 3.5 %copy-start.1 = (bf16[320,896]{1,0:T(8,128)(2,1)S(1)}, bf16[320,896]{1,0:T(8,128)(2,1)}, u32[]{:S(2)}) copy-start(bf16[320,896]{1,0:T(8,128)(2,1)} %get-tuple-element.17) | copy-start | bytes 1720324
  147.0 4.3 %copy-start = (bf16[320,896]{1,0:T(8,128)(2,1)S(1)}, bf16[320,896]{1,0:T(8,128)(2,1)}, u32[]{:S(2)}) copy-start(bf16[320,896]{1,0:T(8,128)(2,1)} %get-tuple-element.18) | copy-start | bytes 1720324

commit v2 on v1

v2 whole, which is shorter than its diff:
```python
import functools

import jax
import jax.numpy as jnp
from jax import lax
from jax.experimental import pallas as pl
from jax.experimental.pallas import tpu as pltpu
from jax.sharding import PartitionSpec as P

MESH = pl.DeviceIdType.MESH
BF16, F32 = jnp.bfloat16, jnp.float32
NY, NZ = 4, 8
CUT = 512


def dot(a, b):
    return jnp.dot(a, b, preferred_element_type=F32)


def dot_last(a, b):
    return lax.dot_general(a, b, (((1,), (1,)), ((), ())), preferred_element_type=F32)


def dot_first(a, b):
    return lax.dot_general(a, b, (((0,), (0,)), ((), ())), preferred_element_type=F32)


def flat(x):
    return x.reshape((-1, x.shape[-1]))


class Links:
    def __init__(self, send, late, recv):
        self.send, self.late, self.recv = send, late, recv
        self.n_send = self.n_recv = 0
        self.started = []

    def slots(self, n=1):
        first = self.n_recv
        self.n_recv += n
        return first

    def copy(self, src, dst, slot, to):
        c = pltpu.make_async_remote_copy(
            src_ref=src,
            dst_ref=dst,
            send_sem=self.send.at[self.n_send],
            recv_sem=self.recv.at[slot],
            device_id=to,
            device_id_type=MESH,
        )
        self.n_send += 1
        return c

    def put(self, src, dst, slot, to):
        c = self.copy(src, dst, slot, to)
        c.start()
        self.started.append((c, None))

    def put_or_keep(self, src, dst, slot, to, away):
        c = self.copy(src, dst, slot, to)

        @pl.when(away == 1)
        def _():
            c.start()

        @pl.when(away == 0)
        def _():
            pltpu.make_async_copy(src, dst, self.recv.at[slot]).start()

        self.started.append((c, away))

    def aside(self, src, dst, slot, to):
        pltpu.make_async_remote_copy(
            src_ref=src,
            dst_ref=dst,
            send_sem=self.late.at[slot - self.late_first],
            recv_sem=self.recv.at[slot],
            device_id=to,
            device_id_type=MESH,
        ).start()

    def aside_sent(self, src, dst, slot, to):
        pltpu.make_async_remote_copy(
            src_ref=src,
            dst_ref=dst,
            send_sem=self.late.at[slot - self.late_first],
            recv_sem=self.recv.at[slot],
            device_id=to,
            device_id_type=MESH,
        ).wait_send()

    def arrived(self, dst, slot):
        pltpu.make_async_copy(dst, dst, self.recv.at[slot]).wait()

    def finish(self, last=0):
        done, self.started = self.started[: len(self.started) - last], self.started[len(self.started) - last :]
        for c, away in done:
            if away is None:
                c.wait_send()
            else:
                pl.when(away == 1)(c.wait_send)


def kernel(
    tok, wg_h, wu_h, wd_h, go, mixed_o, gt_o, gwg_o, gwu_o, gwd_o,
    tok_a, go_a, wg, wu, wd, tok_t, go_t,
    g_p, g_f, g_x, g_s, g_y, u_p, u_f, u_y, u_s, u_x,
    h1_p, h1_f, h1_x, h1_s, h1_y, h2_p, h2_f, h2_y, h2_s, h2_x,
    gate_v, up_v, sig_v, hid_a, gr_a,
    part1, part2, pair1, pair2, zs1, zs2, zr1, zr2, mixed_v, gt_v,
    gw_f, gw_s, gw_r,
    send, late, recv, loc,
):
    row, col, l = lax.axis_index("row"), lax.axis_index("col"), lax.axis_index("dp")
    h, y = row // NY, lax.rem(row, NY)
    z, k = col // 2, lax.rem(col, 2)
    l1 = l + h - 2 * l * h

    def dev(hh, yy, zz, kk, ll):
        return (hh * NY + yy, zz * 2 + kk, ll)

    def ys(d):
        return lax.rem(y + d, NY)

    def zs(d):
        return lax.rem(z + d + NZ, NZ)

    over_y = [None] + [dev(h, ys(d), z, k, l) for d in (1, 2, 3)]
    over_x = dev(1 - h, y, z, k, 1 - l)
    twin = (row, col, 1 - l)
    core = dev(h, y, z, 1 - k, l)

    loads = []
    for i, (src, dst) in enumerate(((wg_h, wg), (wu_h, wu), (wd_h, wd))):
        c = pltpu.make_async_copy(src, dst, loc.at[i])
        c.start()
        loads.append(c)

    barrier = pltpu.get_barrier_semaphore()
    friends = [over_x, twin, core, dev(h, y, z, 1 - k, 1 - l)] + over_y[1:]
    for d in range(1, NZ):
        for ll in (l, 1 - l):
            friends.append(dev(h, y, zs(d), k, ll))
    for to in friends:
        pl.semaphore_signal(barrier, inc=1, device_id=to, device_id_type=MESH)
    pl.semaphore_wait(barrier, len(friends))

    net = Links(send, late, recv)

    side = 1 - 2 * k
    tok_g, go_g = [(dst, net.slots(16)) for dst in (tok_a, go_a)]

    def gather_put(gather, origin, to):
        dst, base = gather
        net.put(dst.at[origin], dst.at[origin], base + origin, to)

    def gather_start(src, gather):
        dst, base = gather
        for to in (dev(h, y, zs(side), k, l1), dev(h, y, zs(-side), k, l1), dev(h, y, z, 1 - k, l1)):
            net.put(src, dst.at[col], base + col, to)
        net.put_or_keep(src, dst.at[col], base + col, dev(h, y, z, k, l1), h)

    def gather_step(gather, step):
        dst, base = gather
        far = zs(-side * step) * 2 + k
        net.arrived(dst.at[far], base + far)
        if step < 4:
            gather_put(gather, far, dev(h, y, zs(side), k, l))
        gather_put(gather, far, core)
        if step < 4:
            near = zs(side * step) * 2 + k
            net.arrived(dst.at[near], base + near)
            if step < 3:
                gather_put(gather, near, dev(h, y, zs(-side), k, l))
            gather_put(gather, near, core)

    def gathered(gather, zz):
        dst, base = gather
        if zz is z:
            net.arrived(dst.at[col], base + col)
        other = zz * 2 + 1 - k
        net.arrived(dst.at[other], base + other)
        return flat(dst[pl.ds(zz * 2, 2)])

    def x_first_block(out, zz, sums):
        f, p, x, slot = sums
        hi, yi = zz // NY, lax.rem(zz, NY)

        @pl.when(hi == h)
        def _():
            f[yi] = out

        @pl.when(hi != h)
        def _():
            p[yi] = out.astype(BF16)
            net.aside(p.at[yi], x.at[yi], slot + yi, over_x)

    def x_first_pass(f, x, s, yr, slot):
        first = net.slots(3)
        for d in (2, 1, 3):
            i = ys(d)
            net.arrived(x.at[i], slot + i)
            s[i] = (f[i] + x[i].astype(F32)).astype(BF16)
            net.put(s.at[i], yr.at[d - 1], first + d - 1, over_y[d])
        net.arrived(x.at[y], slot + y)
        return first

    def x_first_sum(f, x, yr, slot):
        total = f[y] + x[y].astype(F32)
        for d in (1, 3, 2):
            net.arrived(yr.at[d - 1], slot + d - 1)
            total = total + yr[d - 1].astype(F32)
        return total

    def y_first_block(out, zz, sums):
        f, p, yr, slot = sums
        hi, yi = zz // NY, lax.rem(zz, NY)
        f[hi, yi] = out

        @pl.when(yi != y)
        def _():
            p[hi, yi] = out.astype(BF16)
            d = lax.rem(yi - y + NY, NY) - 1
            net.aside(p.at[hi, yi], yr.at[d, hi], slot + 2 * d + hi, dev(h, yi, z, k, l))

    def y_first_pass(f, yr, s, x, slot):
        total = f[1 - h, y]
        for d in (1, 3, 2):
            net.arrived(yr.at[d - 1, 1 - h], slot + 2 * (d - 1) + 1 - h)
            total = total + yr[d - 1, 1 - h].astype(F32)
        s[...] = total.astype(BF16)
        first = net.slots()
        net.put(s, x, first, over_x)
        return first

    def y_first_sum(f, yr, x, slot1, slot2):
        total = f[h, y]
        for d in (1, 3, 2):
            net.arrived(yr.at[d - 1, h], slot1 + 2 * (d - 1) + h)
            total = total + yr[d - 1, h].astype(F32)
        net.arrived(x, slot2)
        return total + x[...].astype(F32)

    net.late_first = net.n_recv
    g1, u1, h11, h21 = net.slots(4), net.slots(6), net.slots(4), net.slots(6)

    def block_gu(zz):
        a = gathered(tok_g, zz)
        y_first_block(dot(a, wu[...]), zz, (u_f, u_p, u_y, u1))
        x_first_block(dot(a, wg[...]), zz, (g_f, g_p, g_x, g1))

    def block_h(zz):
        a = gathered(go_g, zz)
        y_first_block(dot_last(a, wd[CUT:]), zz, (h2_f, h2_p, h2_y, h21))
        x_first_block(dot_last(a, wd[:CUT]), zz, (h1_f, h1_p, h1_x, h11))

    def chips(step):
        return (zs(-side * step), zs(side * step)) if step < 4 else (zs(4),)

    gather_start(tok, tok_g)
    for c in loads:
        c.wait()
    gather_step(tok_g, 1)
    gather_start(go, go_g)
    block_gu(z)
    for step in (2, 3, 4):
        gather_step(tok_g, step)
        gather_step(go_g, step - 1)
        for zz in chips(step - 1):
            block_gu(zz)
    gather_step(go_g, 4)
    block_gu(zs(4))
    block_h(z)
    for zz in chips(1):
        block_h(zz)
    g2 = x_first_pass(g_f, g_x, g_s, g_y, g1)
    u2 = y_first_pass(u_f, u_y, u_s, u_x, u1)
    for step in (2, 3, 4):
        for zz in chips(step):
            block_h(zz)
    tok_t[...] = flat(tok_a[...]).T
    gate = x_first_sum(g_f, g_x, g_y, g2)
    up = y_first_sum(u_f, u_y, u_x, u1, u2)
    sig = jax.nn.sigmoid(gate)
    gate_v[...] = gate
    up_v[...] = up
    sig_v[...] = sig
    hid_a[0, h, y] = (gate * sig * up).astype(BF16)

    class Spread:
        def __init__(self, buf, lo, hi):
            self.buf, self.cols = buf, pl.ds(lo, hi - lo)
            self.base = net.slots(10)
            self.put(h, y, over_x)
            self.put(h, y, over_y[1])
            self.put(h, y, over_y[3])

        def at(self, hh, yy, half=None):
            rows = pl.ds(0, 96) if half is None else pl.ds(48 * half, 48)
            return self.buf.at[:, hh, yy, rows, self.cols]

        def slot(self, hh, yy, half=None):
            return self.base + (8 + hh if half == 1 else hh * NY + yy)

        def put(self, hh, yy, to, half=None):
            ref = self.at(hh, yy, half)
            net.put(ref, ref, self.slot(hh, yy, half), to)

        def wait(self, hh, yy, half=None):
            net.arrived(self.at(hh, yy, half), self.slot(hh, yy, half))

        def across(self, hh, also_x=False):
            for d, half in ((3, 0), (1, 1)):
                self.wait(hh, ys(d))
                self.put(hh, ys(d), over_y[4 - d], half)
                if also_x:
                    self.put(hh, ys(d), over_x)

    class XThenY(Spread):
        def relay1(self):
            self.wait(1 - h, y)
            self.put(1 - h, y, over_y[1])
            self.put(1 - h, y, over_y[3])

        def relay2(self):
            self.across(h)

        def relay3(self):
            self.across(1 - h)

        def rest(self):
            for hh in (h, 1 - h):
                for half in (0, 1):
                    self.wait(hh, ys(2), half)

    class YThenX(Spread):
        def relay1(self):
            self.across(h, True)

        def relay2(self):
            for half in (0, 1):
                self.wait(h, ys(2), half)
                self.put(h, ys(2), over_x, half)

        def rest(self):
            for d in (0, 1, 3):
                self.wait(1 - h, ys(d))
            for half in (0, 1):
                self.wait(1 - h, ys(2), half)

    width = hid_a.shape[-1]
    hid0 = XThenY(hid_a, 0, CUT)
    hid1 = YThenX(hid_a, CUT, width)
    h12 = x_first_pass(h1_f, h1_x, h1_s, h1_y, h11)
    h22 = y_first_pass(h2_f, h2_y, h2_s, h2_x, h21)
    go_t[...] = flat(go_a[...]).T
    hid0.relay1()
    hid1.relay1()
    hid0.relay2()

    def grads(at, total):
        gate, up, sig = gate_v[:, at], up_v[:, at], sig_v[:, at]
        gr_a[1, h, y, :, at] = (total * gate * sig).astype(BF16)
        gr_a[0, h, y, :, at] = (total * up * sig * (1.0 + gate * (1.0 - sig))).astype(BF16)

    grads(pl.ds(0, CUT), x_first_sum(h1_f, h1_x, h1_y, h12))
    gr0 = XThenY(gr_a, 0, CUT)
    grads(pl.ds(CUT, width - CUT), y_first_sum(h2_f, h2_y, h2_x, h21, h22))
    gr1 = YThenX(gr_a, CUT, width)
    hid1.relay2()
    hid0.relay3()
    gr0.relay1()

    def weight_grad(left, buf, first, lo, hi, mine):
        at, to = pl.ds(lo, hi - lo), pl.ds(first + lo, hi - lo)
        base = (l if mine else 1 - l) * 320
        right = buf[:, :, :, at].reshape((8 * 96, hi - lo))
        for q in range(2):
            out = dot(left[pl.ds(pl.multiple_of(base + q * 160, 32), 160)], right)
            if mine:
                gw_f[pl.ds(q * 160, 160), to] = out
            else:
                gw_s[pl.ds(q * 160, 160), to] = out.astype(BF16)
        if not mine:
            slot = net.slots()
            net.put(gw_s.at[:, to], gw_r.at[:, to], slot, twin)
            return slot, to

    def weight_out(out, lo, hi, sent):
        slot, at = sent
        net.arrived(gw_r.at[:, at], slot)
        out[:, pl.ds(lo, hi - lo)] = (gw_f[:, at] + gw_r[:, at].astype(F32)).astype(BF16)

    def pair_send(part, pair, lo, hi):
        slot, at = net.slots(), pl.ds(lo, hi - lo)
        net.put(part.at[at, 1 - k], pair.at[at], slot, core)
        return slot, at

    def pair_pass(part, pair, zsend, zrecv, sent):
        for slot, at in sent:
            net.arrived(pair.at[at], slot)
        for zz in range(NZ):
            zsend[zz] = (part[zz, k] + pair[zz]).astype(BF16)
        slot = net.slots(NZ)
        for d in (4, 3, 5, 2, 6, 1, 7):
            net.put(zsend.at[zs(d)], zrecv.at[d], slot + d, dev(h, y, zs(d), k, l))
        return slot

    def z_sum(part, pair, zrecv, slot, out):
        total = part[z, k] + pair[z]
        for d in (1, 7, 2, 6, 3, 5, 4):
            net.arrived(zrecv.at[d], slot + d)
            total = total + zrecv[d].astype(F32)
        zrecv[0] = total.astype(BF16)
        net.put_or_keep(zrecv.at[0], out, slot, twin, h)
        return out, slot

    def rows4(buf, i, at):
        return buf[i // 2, pl.ds(2 * (i % 2), 2), :, at].reshape((192, -1))

    hid, gg, gu = hid_a.at[0], gr_a.at[0], gr_a.at[1]
    hid0.rest()
    hid1.rest()
    dw = weight_grad(go_t, hid, 2 * width, 0, width, False)
    gr1.relay1()
    gr0.relay2()
    gr1.relay2()
    gr0.relay3()
    sent = []
    for i in range(4):
        part1[pl.ds(2 * i, 2)] = dot(rows4(hid, i, pl.ds(0, width)), wd[...]).reshape((2, 2, 48, -1))
        sent.append(pair_send(part1, pair1, 2 * i, 2 * i + 2))
    gr0.rest()
    wg0 = weight_grad(tok_t, gg, 0, 0, CUT, False)
    m2 = pair_pass(part1, pair1, zs1, zr1, sent)
    wu0 = weight_grad(tok_t, gu, width, 0, CUT, False)

    def token_grad(i, lo, hi):
        at = pl.ds(lo, hi - lo)
        out = dot_last(rows4(gg, i, at), wg[:, at]) + dot_last(rows4(gu, i, at), wu[:, at])
        return out.reshape((2, 2, 48, -1))

    for i in range(4):
        part2[pl.ds(2 * i, 2)] = token_grad(i, 0, CUT)
    gr1.rest()
    sent = []
    for i in range(4):
        part2[pl.ds(2 * i, 2)] += token_grad(i, CUT, width)
        sent.append(pair_send(part2, pair2, 2 * i, 2 * i + 2))
    wg1 = weight_grad(tok_t, gg, 0, CUT, width, False)
    wu1 = weight_grad(tok_t, gu, width, CUT, width, False)
    t2 = pair_pass(part2, pair2, zs2, zr2, sent)
    for first, n, p, x in (
        (g1, 4, g_p.at[0], g_x.at[0]),
        (u1, 6, u_p.at[0, 0], u_y.at[0, 0]),
        (h11, 4, h1_p.at[0], h1_x.at[0]),
        (h21, 6, h2_p.at[0, 0], h2_y.at[0, 0]),
    ):
        for i in range(n):
            net.aside_sent(p, x, first + i, over_x)
    net.finish(25)
    weight_grad(go_t, hid, 2 * width, 0, width, True)
    weight_out(gwd_o, 0, width, dw)
    mixed = z_sum(part1, pair1, zr1, m2, mixed_v)
    weight_grad(tok_t, gg, 0, 0, width, True)
    weight_grad(tok_t, gu, width, 0, width, True)
    weight_out(gwg_o, 0, CUT, wg0)
    weight_out(gwu_o, 0, CUT, wu0)
    grad = z_sum(part2, pair2, zr2, t2, gt_v)
    weight_out(gwg_o, CUT, width, wg1)
    weight_out(gwu_o, CUT, width, wu1)
    for o, (v, slot) in ((mixed_o, mixed), (gt_o, grad)):
        net.arrived(v, slot)
        o[...] = v[...]
    net.finish()


def copy_out(*refs):
    for i in range(5):
        refs[5 + i][...] = refs[i][...]


def per_device(tokens, w_gate, w_up, w_down, grad_out):
    n_tok, d = tokens.shape
    f = w_gate.shape[1]
    rest = f - CUT

    def x_first(w):
        return [
            pltpu.VMEM((4, 96, w), BF16),
            pltpu.VMEM((4, 96, w), F32),
            pltpu.VMEM((4, 96, w), BF16),
            pltpu.VMEM((4, 96, w), BF16),
            pltpu.VMEM((3, 96, w), BF16),
        ]

    def y_first(w):
        return [
            pltpu.VMEM((2, 4, 96, w), BF16),
            pltpu.VMEM((2, 4, 96, w), F32),
            pltpu.VMEM((3, 2, 96, w), BF16),
            pltpu.VMEM((96, w), BF16),
            pltpu.VMEM((96, w), BF16),
        ]

    scratch = [
        pltpu.VMEM((16, n_tok, d), BF16),
        pltpu.VMEM((16, n_tok, d), BF16),
        pltpu.VMEM(w_gate.shape, BF16),
        pltpu.VMEM(w_up.shape, BF16),
        pltpu.VMEM(w_down.shape, BF16),
        *[pltpu.VMEM((d, 16 * n_tok), BF16)] * 2,
        *x_first(f),
        *y_first(f),
        *x_first(CUT),
        *y_first(rest),
        *[pltpu.VMEM((96, f), F32)] * 3,
        pltpu.VMEM((1, 2, 4, 96, f), BF16),
        pltpu.VMEM((2, 2, 4, 96, f), BF16),
        *[pltpu.VMEM((8, 2, n_tok, d), F32)] * 2,
        *[pltpu.VMEM((8, n_tok, d), F32)] * 2,
        *[pltpu.VMEM((8, n_tok, d), BF16)] * 4,
        *[pltpu.VMEM((n_tok, d), BF16)] * 2,
        pltpu.VMEM((d // 2, 3 * f), F32),
        pltpu.VMEM((d // 2, 3 * f), BF16),
        pltpu.VMEM((d // 2, 3 * f), BF16),
        pltpu.SemaphoreType.DMA((160,)),
        pltpu.SemaphoreType.DMA((20,)),
        pltpu.SemaphoreType.DMA((160,)),
        pltpu.SemaphoreType.DMA((3,)),
    ]
    vmem, hbm = pl.BlockSpec(memory_space=pltpu.VMEM), pl.BlockSpec(memory_space=pl.ANY)
    results = pl.pallas_call(
        kernel,
        out_shape=(
            jax.ShapeDtypeStruct((n_tok, d), BF16),
            jax.ShapeDtypeStruct((n_tok, d), BF16),
            jax.ShapeDtypeStruct((d // 2, f), BF16),
            jax.ShapeDtypeStruct((d // 2, f), BF16),
            jax.ShapeDtypeStruct((d // 2, f), BF16),
        ),
        in_specs=[vmem, hbm, hbm, hbm, vmem],
        out_specs=(vmem,) * 5,
        scratch_shapes=scratch,
        compiler_params=pltpu.CompilerParams(
            collective_id=0, has_side_effects=True, vmem_limit_bytes=62 * 2**20
        ),
        name="swiglu",
    )(tokens, w_gate, w_up, w_down, grad_out)
    mixed, grad_tokens, grad_gate, grad_up, grad_down = pl.pallas_call(
        copy_out,
        out_shape=tuple(jax.ShapeDtypeStruct(r.shape, r.dtype) for r in results),
        in_specs=[vmem] * 5,
        out_specs=(vmem,) * 5,
        name="copy_out",
    )(*results)
    return mixed, grad_tokens, grad_gate, grad_up, grad_down.T


def solution(mesh):
    placed = (
        P(("col", "dp"), "row"),
        P("row", "col"),
        P("row", "col"),
        P("col", "row"),
        P(("col", "dp"), "row"),
    )
    return jax.shard_map(
        per_device,
        mesh=mesh,
        in_specs=placed,
        out_specs=(
            P(("col", "dp"), "row"),
            P(("col", "dp"), "row"),
            P(("row", "dp"), "col"),
            P(("row", "dp"), "col"),
            P("col", ("row", "dp")),
        ),
        check_vma=False,
    )
```

time: 152 us -> 122 us (0.80)
  Pallas kernels: 146 us -> 122 us
  local copies, waits for them, and re-layouts: 5.14 us -> 0 us
    pallas_call x1, Pallas kernels: 146 us -> 119 us  [per_device(): pl.pallas_call(kernel, out_shape=(jax.ShapeDtypeStruct((n_tok, d), BF16),...]
    unnamed x12 -> x0, local copies, waits for them, and re-layouts: 2.88 us -> none
    pallas_call x0 -> x1, Pallas kernels: none -> 2.73 us  [per_device(): pl.pallas_call(copy_out, out_shape=tuple((jax.ShapeDtypeStruct(r.shape, r...]
    pallas_call x1 -> x0, local copies, waits for them, and re-layouts: 2.26 us -> none  [per_device(): pl.pallas_call(kernel, out_shape=(jax.ShapeDtypeStruct((n_tok, d), BF16),...]
where the time goes in v2:
time: 122 us
  Pallas kernels  122 us (100%)
    pallas_call x1, Pallas kernels, per_device(): pl.pallas_call(kernel, out_shape=(jax.ShapeDtypeStruct((n_tok, d), BF16),...  119 us
    pallas_call x1, Pallas kernels, per_device(): pl.pallas_call(copy_out, out_shape=tuple((jax.ShapeDtypeStruct(r.shape, r...  2.73 us

profile of v2, /device:TPU:4, one launch (start us, length us, event | category | flops | bytes accessed | tf_op | source)
XLA Modules:
  0.0 122.2 jit_solution(4401115440226619115)
XLA Ops:
  0.6 118.8 %swiglu.1 = (bf16[48,640]{1,0:T(8,128)(2,1)}, bf16[48,640]{1,0:T(8,128)(2,1)}, bf16[320,896]{1,0:T(8,128)(2,1)}, bf16[320,896]{1,0:T(8,128)(2,1)}, bf16[320,896]{1,0:T(8,128)(2,1)}) custom-call(bf16[48,640]{1,0:T(8,128)(2,1)} %tok.1, bf16[640,896]{1,0:T(8,128)(2,1)} %wg_h.1, bf16[640,896]{1,0:T(8,128)(2,1)} %wu_h.1, bf16[896,640]{1,0:T(8,128)(2,1)} %wd_h.1, ...), custom_call_target="tpu_custom_call" | custom-call | tf_op jit(solution)/shard_map/swiglu/pallas_call | solution.py:534
  119.5 2.7 %copy_out.1 = (bf16[48,640]{1,0:T(8,128)(2,1)}, bf16[48,640]{1,0:T(8,128)(2,1)}, bf16[320,896]{1,0:T(8,128)(2,1)}, bf16[320,896]{1,0:T(8,128)(2,1)}, bf16[320,896]{1,0:T(8,128)(2,1)}) custom-call(bf16[48,640]{1,0:T(8,128)(2,1)} %get-tuple-element.15.refs_0_, bf16[48,640]{1,0:T(8,128)(2,1)} %get-tuple-element.16.refs_1_, ...), custom_call_target="tpu_custom_call" | custom-call | tf_op jit(solution)/shard_map/copy_out/pallas_call | solution.py:551

commit v3 on v2

--- a/solution.py
+++ b/solution.py
@@ -70,21 +70,21 @@
 
         self.started.append((c, away))
 
-    def aside(self, src, dst, slot, to):
+    def aside(self, src, dst, slot, to, sem=None):
         pltpu.make_async_remote_copy(
             src_ref=src,
             dst_ref=dst,
-            send_sem=self.late.at[slot - self.late_first],
+            send_sem=self.late.at[slot - self.late_first if sem is None else sem],
             recv_sem=self.recv.at[slot],
             device_id=to,
             device_id_type=MESH,
         ).start()
 
-    def aside_sent(self, src, dst, slot, to):
+    def aside_sent(self, src, dst, slot, to, sem=None):
         pltpu.make_async_remote_copy(
             src_ref=src,
             dst_ref=dst,
-            send_sem=self.late.at[slot - self.late_first],
+            send_sem=self.late.at[slot - self.late_first if sem is None else sem],
             recv_sem=self.recv.at[slot],
             device_id=to,
             device_id_type=MESH,
@@ -115,7 +115,6 @@
     row, col, l = lax.axis_index("row"), lax.axis_index("col"), lax.axis_index("dp")
     h, y = row // NY, lax.rem(row, NY)
     z, k = col // 2, lax.rem(col, 2)
-    l1 = l + h - 2 * l * h
 
     def dev(hh, yy, zz, kk, ll):
         return (hh * NY + yy, zz * 2 + kk, ll)
@@ -138,10 +137,9 @@
         loads.append(c)
 
     barrier = pltpu.get_barrier_semaphore()
-    friends = [over_x, twin, core, dev(h, y, z, 1 - k, 1 - l)] + over_y[1:]
-    for d in range(1, NZ):
-        for ll in (l, 1 - l):
-            friends.append(dev(h, y, zs(d), k, ll))
+    friends = [over_x, twin, core] + over_y[1:]
+    for d in (1, 2, 6, 7):
+        friends.append(dev(h, y, zs(d), k, l))
     for to in friends:
         pl.semaphore_signal(barrier, inc=1, device_id=to, device_id_type=MESH)
     pl.semaphore_wait(barrier, len(friends))
@@ -157,28 +155,37 @@
 
     def gather_start(src, gather):
         dst, base = gather
-        for to in (dev(h, y, zs(side), k, l1), dev(h, y, zs(-side), k, l1), dev(h, y, z, 1 - k, l1)):
-            net.put(src, dst.at[col], base + col, to)
-        net.put_or_keep(src, dst.at[col], base + col, dev(h, y, z, k, l1), h)
-
-    def gather_step(gather, step):
+        net.put_or_keep(src, dst.at[col], base + col, twin, h)
+
+    def gather_share(gather):
         dst, base = gather
-        far = zs(-side * step) * 2 + k
-        net.arrived(dst.at[far], base + far)
-        if step < 4:
-            gather_put(gather, far, dev(h, y, zs(side), k, l))
-        gather_put(gather, far, core)
-        if step < 4:
-            near = zs(side * step) * 2 + k
-            net.arrived(dst.at[near], base + near)
-            if step < 3:
-                gather_put(gather, near, dev(h, y, zs(-side), k, l))
-            gather_put(gather, near, core)
+        net.arrived(dst.at[col], base + col)
+        gather_put(gather, col, core)
+        for d in (2 * side, -2 * side, side, -side):
+            gather_put(gather, col, dev(h, y, zs(d), k, l))
+
+    def gather_pass(gather, steps, targets):
+        origin = zs(steps) * 2 + k
+        dst, base = gather
+        net.arrived(dst.at[origin], base + origin)
+        for d in targets:
+            gather_put(gather, origin, dev(h, y, zs(d), k, l))
+        gather_put(gather, origin, core)
+
+    def gather_two(gather):
+        gather_pass(gather, -2 * side, (2 * side, side))
+        gather_pass(gather, 2 * side, (-side,))
+
+    def gather_one(gather):
+        gather_pass(gather, -side, ())
+        gather_pass(gather, side, ())
+
+    def gather_rest(gather):
+        for d in (-3 * side, 3 * side, 4):
+            gather_pass(gather, d, ())
 
     def gathered(gather, zz):
         dst, base = gather
-        if zz is z:
-            net.arrived(dst.at[col], base + col)
         other = zz * 2 + 1 - k
         net.arrived(dst.at[other], base + other)
         return flat(dst[pl.ds(zz * 2, 2)])
@@ -206,6 +213,21 @@
         net.arrived(x.at[y], slot + y)
         return first
 
+    def x_first_relay(zz, sums, to):
+        f, p, x, slot = sums
+        s, yr, first, sem = to
+        hi, yi = zz // NY, lax.rem(zz, NY)
+
+        @pl.when(hi == h)
+        def _():
+            net.arrived(x.at[yi], slot + yi)
+
+            @pl.when(yi != y)
+            def _():
+                d = lax.rem(yi - y + NY, NY) - 1
+                s[yi] = (f[yi] + x[yi].astype(F32)).astype(BF16)
+                net.aside(s.at[yi], yr.at[d], first + d, dev(h, yi, z, k, l), sem + d)
+
     def x_first_sum(f, x, yr, slot):
         total = f[y] + x[y].astype(F32)
         for d in (1, 3, 2):
@@ -244,12 +266,16 @@
 
     net.late_first = net.n_recv
     g1, u1, h11, h21 = net.slots(4), net.slots(6), net.slots(4), net.slots(6)
+    g2 = net.slots(3)
 
     def block_gu(zz):
         a = gathered(tok_g, zz)
         y_first_block(dot(a, wu[...]), zz, (u_f, u_p, u_y, u1))
         x_first_block(dot(a, wg[...]), zz, (g_f, g_p, g_x, g1))
 
+    def relay_g(zz):
+        x_first_relay(zz, (g_f, g_p, g_x, g1), (g_s, g_y, g2, 36))
+
     def block_h(zz):
         a = gathered(go_g, zz)
         y_first_block(dot_last(a, wd[CUT:]), zz, (h2_f, h2_p, h2_y, h21))
@@ -259,26 +285,35 @@
         return (zs(-side * step), zs(side * step)) if step < 4 else (zs(4),)
 
     gather_start(tok, tok_g)
+    gather_share(tok_g)
+    gather_start(go, go_g)
     for c in loads:
         c.wait()
-    gather_step(tok_g, 1)
-    gather_start(go, go_g)
     block_gu(z)
-    for step in (2, 3, 4):
-        gather_step(tok_g, step)
-        gather_step(go_g, step - 1)
-        for zz in chips(step - 1):
-            block_gu(zz)
-    gather_step(go_g, 4)
-    block_gu(zs(4))
-    block_h(z)
-    for zz in chips(1):
-        block_h(zz)
-    g2 = x_first_pass(g_f, g_x, g_s, g_y, g1)
+    gather_two(tok_g)
+    gather_one(tok_g)
+    for zz in chips(1) + chips(2):
+        block_gu(zz)
+    gather_rest(tok_g)
+    gather_share(go_g)
+    for zz in chips(3) + chips(4):
+        block_gu(zz)
+    for zz in (z,) + chips(1):
+        relay_g(zz)
+    gather_two(go_g)
+    for zz in chips(2) + chips(3):
+        relay_g(zz)
+    gather_one(go_g)
+    gather_rest(go_g)
+
+    def h_blocks(lo, hi):
+        for zz in ((z,) + chips(1) + chips(2) + chips(3) + chips(4))[lo:hi]:
+            block_h(zz)
+
+    h_blocks(0, 3)
+    relay_g(zs(4))
     u2 = y_first_pass(u_f, u_y, u_s, u_x, u1)
-    for step in (2, 3, 4):
-        for zz in chips(step):
-            block_h(zz)
+    h_blocks(3, 8)
     tok_t[...] = flat(tok_a[...]).T
     gate = x_first_sum(g_f, g_x, g_y, g2)
     up = y_first_sum(u_f, u_y, u_x, u1, u2)
@@ -350,27 +385,12 @@
                 self.wait(1 - h, ys(2), half)
 
     width = hid_a.shape[-1]
-    hid0 = XThenY(hid_a, 0, CUT)
-    hid1 = YThenX(hid_a, CUT, width)
-    h12 = x_first_pass(h1_f, h1_x, h1_s, h1_y, h11)
-    h22 = y_first_pass(h2_f, h2_y, h2_s, h2_x, h21)
-    go_t[...] = flat(go_a[...]).T
-    hid0.relay1()
-    hid1.relay1()
-    hid0.relay2()
+    hid, gg, gu = hid_a.at[0], gr_a.at[0], gr_a.at[1]
 
     def grads(at, total):
         gate, up, sig = gate_v[:, at], up_v[:, at], sig_v[:, at]
         gr_a[1, h, y, :, at] = (total * gate * sig).astype(BF16)
         gr_a[0, h, y, :, at] = (total * up * sig * (1.0 + gate * (1.0 - sig))).astype(BF16)
-
-    grads(pl.ds(0, CUT), x_first_sum(h1_f, h1_x, h1_y, h12))
-    gr0 = XThenY(gr_a, 0, CUT)
-    grads(pl.ds(CUT, width - CUT), y_first_sum(h2_f, h2_y, h2_x, h21, h22))
-    gr1 = YThenX(gr_a, CUT, width)
-    hid1.relay2()
-    hid0.relay3()
-    gr0.relay1()
 
     def weight_grad(left, buf, first, lo, hi, mine):
         at, to = pl.ds(lo, hi - lo), pl.ds(first + lo, hi - lo)
@@ -397,17 +417,28 @@
         net.put(part.at[at, 1 - k], pair.at[at], slot, core)
         return slot, at
 
-    def pair_pass(part, pair, zsend, zrecv, sent):
-        for slot, at in sent:
-            net.arrived(pair.at[at], slot)
+    def pair_pass(sums, sent, i, first_sem):
+        part, pair, zsend, zrecv, base = sums
+        slot, at = sent
+        net.arrived(pair.at[at], slot)
+        for zz in (2 * i, 2 * i + 1):
+            zsend[zz] = (part[zz, k] + pair[zz]).astype(BF16)
+            d = lax.rem(zz - z + NZ, NZ)
+
+            @pl.when(d != 0)
+            def _():
+                net.aside(zsend.at[zz], zrecv.at[d], base + d, dev(h, y, zz, k, l), first_sem + zz)
+
+    def pair_sent(sums, first_sem):
+        part, pair, zsend, zrecv, base = sums
         for zz in range(NZ):
-            zsend[zz] = (part[zz, k] + pair[zz]).astype(BF16)
-        slot = net.slots(NZ)
-        for d in (4, 3, 5, 2, 6, 1, 7):
-            net.put(zsend.at[zs(d)], zrecv.at[d], slot + d, dev(h, y, zs(d), k, l))
-        return slot
-
-    def z_sum(part, pair, zrecv, slot, out):
+
+            @pl.when(zz != z)
+            def _():
+                net.aside_sent(zsend.at[zz], zrecv.at[0], base, twin, first_sem + zz)
+
+    def z_sum(sums, out):
+        part, pair, zsend, zrecv, slot = sums
         total = part[z, k] + pair[z]
         for d in (1, 7, 2, 6, 3, 5, 4):
             net.arrived(zrecv.at[d], slot + d)
@@ -419,38 +450,79 @@
     def rows4(buf, i, at):
         return buf[i // 2, pl.ds(2 * (i % 2), 2), :, at].reshape((192, -1))
 
-    hid, gg, gu = hid_a.at[0], gr_a.at[0], gr_a.at[1]
-    hid0.rest()
-    hid1.rest()
-    dw = weight_grad(go_t, hid, 2 * width, 0, width, False)
-    gr1.relay1()
-    gr0.relay2()
-    gr1.relay2()
-    gr0.relay3()
-    sent = []
-    for i in range(4):
-        part1[pl.ds(2 * i, 2)] = dot(rows4(hid, i, pl.ds(0, width)), wd[...]).reshape((2, 2, 48, -1))
-        sent.append(pair_send(part1, pair1, 2 * i, 2 * i + 2))
-    gr0.rest()
-    wg0 = weight_grad(tok_t, gg, 0, 0, CUT, False)
-    m2 = pair_pass(part1, pair1, zs1, zr1, sent)
-    wu0 = weight_grad(tok_t, gu, width, 0, CUT, False)
-
     def token_grad(i, lo, hi):
         at = pl.ds(lo, hi - lo)
         out = dot_last(rows4(gg, i, at), wg[:, at]) + dot_last(rows4(gu, i, at), wu[:, at])
         return out.reshape((2, 2, 48, -1))
 
+    sums1 = part1, pair1, zs1, zr1, net.slots(NZ)
+    sums2 = part2, pair2, zs2, zr2, net.slots(NZ)
+
+    def mixed_parts():
+        sent = []
+        for i in range(4):
+            out = dot(rows4(hid, i, pl.ds(0, width)), wd[...])
+            part1[pl.ds(2 * i, 2)] = out.reshape((2, 2, 48, -1))
+            sent.append(pair_send(part1, pair1, 2 * i, 2 * i + 2))
+        return sent
+
+    def mixed_pass():
+        for i in range(4):
+            pair_pass(sums1, sent1[i], i, 20)
+
+    def token_parts():
+        sent = []
+        for i in range(4):
+            part2[pl.ds(2 * i, 2)] += token_grad(i, CUT, width)
+            sent.append(pair_send(part2, pair2, 2 * i, 2 * i + 2))
+            if i > 1:
+                pair_pass(sums2, sent[i - 2], i - 2, 28)
+        pair_pass(sums2, sent[2], 2, 28)
+        pair_pass(sums2, sent[3], 3, 28)
+
+    hid0 = XThenY(hid_a, 0, CUT)
+    hid1 = YThenX(hid_a, CUT, width)
+    h12 = x_first_pass(h1_f, h1_x, h1_s, h1_y, h11)
+    h22 = y_first_pass(h2_f, h2_y, h2_s, h2_x, h21)
+    go_t[...] = flat(go_a[...]).T
+    hid0.relay1()
+    hid1.relay1()
+    hid0.relay2()
+    grads(pl.ds(0, CUT), x_first_sum(h1_f, h1_x, h1_y, h12))
+    gr0 = XThenY(gr_a, 0, 256)
+    gr1 = YThenX(gr_a, 256, CUT)
+    grads(pl.ds(CUT, width - CUT), y_first_sum(h2_f, h2_y, h2_x, h21, h22))
+    hid1.relay2()
+    hid0.relay3()
+    gr0.relay1()
+    hid0.rest()
+    dw0 = weight_grad(go_t, hid, 2 * width, 0, CUT, False)
+    hid1.rest()
+    dw1 = weight_grad(go_t, hid, 2 * width, CUT, width, False)
+    gr1.relay1()
+    gr0.relay2()
+    gr2 = XThenY(gr_a, CUT, 768)
+    gr3 = YThenX(gr_a, 768, width)
+    gr1.relay2()
+    gr0.relay3()
+    sent1 = mixed_parts()
+    gr2.relay1()
+    gr3.relay1()
+    gr2.relay2()
+    mixed_pass()
+    gr0.rest()
+    gr1.rest()
+    wg0 = weight_grad(tok_t, gg, 0, 0, CUT, False)
+    wu0 = weight_grad(tok_t, gu, width, 0, CUT, False)
+    gr3.relay2()
+    gr2.relay3()
     for i in range(4):
         part2[pl.ds(2 * i, 2)] = token_grad(i, 0, CUT)
-    gr1.rest()
-    sent = []
-    for i in range(4):
-        part2[pl.ds(2 * i, 2)] += token_grad(i, CUT, width)
-        sent.append(pair_send(part2, pair2, 2 * i, 2 * i + 2))
+    gr2.rest()
+    gr3.rest()
+    token_parts()
     wg1 = weight_grad(tok_t, gg, 0, CUT, width, False)
     wu1 = weight_grad(tok_t, gu, width, CUT, width, False)
-    t2 = pair_pass(part2, pair2, zs2, zr2, sent)
     for first, n, p, x in (
         (g1, 4, g_p.at[0], g_x.at[0]),
         (u1, 6, u_p.at[0, 0], u_y.at[0, 0]),
@@ -459,20 +531,25 @@
     ):
         for i in range(n):
             net.aside_sent(p, x, first + i, over_x)
-    net.finish(25)
+    for d in range(3):
+        net.aside_sent(g_s.at[0], g_y.at[0], g2, over_x, 36 + d)
+    pair_sent(sums1, 20)
+    net.finish(20)
     weight_grad(go_t, hid, 2 * width, 0, width, True)
-    weight_out(gwd_o, 0, width, dw)
-    mixed = z_sum(part1, pair1, zr1, m2, mixed_v)
+    weight_out(gwd_o, 0, CUT, dw0)
+    weight_out(gwd_o, CUT, width, dw1)
+    mixed = z_sum(sums1, mixed_v)
     weight_grad(tok_t, gg, 0, 0, width, True)
     weight_grad(tok_t, gu, width, 0, width, True)
     weight_out(gwg_o, 0, CUT, wg0)
     weight_out(gwu_o, 0, CUT, wu0)
-    grad = z_sum(part2, pair2, zr2, t2, gt_v)
+    grad = z_sum(sums2, gt_v)
     weight_out(gwg_o, CUT, width, wg1)
     weight_out(gwu_o, CUT, width, wu1)
     for o, (v, slot) in ((mixed_o, mixed), (gt_o, grad)):
         net.arrived(v, slot)
         o[...] = v[...]
+    pair_sent(sums2, 28)
     net.finish()
 
 
@@ -525,9 +602,9 @@
         pltpu.VMEM((d // 2, 3 * f), F32),
         pltpu.VMEM((d // 2, 3 * f), BF16),
         pltpu.VMEM((d // 2, 3 * f), BF16),
-        pltpu.SemaphoreType.DMA((160,)),
-        pltpu.SemaphoreType.DMA((20,)),
-        pltpu.SemaphoreType.DMA((160,)),
+        pltpu.SemaphoreType.DMA((200,)),
+        pltpu.SemaphoreType.DMA((40,)),
+        pltpu.SemaphoreType.DMA((200,)),
         pltpu.SemaphoreType.DMA((3,)),
     ]
     vmem, hbm = pl.BlockSpec(memory_space=pltpu.VMEM), pl.BlockSpec(memory_space=pl.ANY)

time: 122 us -> 117 us (0.959)
  Pallas kernels: 122 us -> 116 us
    pallas_call x1, Pallas kernels: 119 us -> 113 us  [per_device(): pl.pallas_call(kernel, out_shape=(jax.ShapeDtypeStruct((n_tok, d), BF16),...]
where the time goes in v3:
time: 117 us; the launch traced here: 116 us
  Pallas kernels  116 us (99%)
    pallas_call x1, Pallas kernels, per_device(): pl.pallas_call(kernel, out_shape=(jax.ShapeDtypeStruct((n_tok, d), BF16),...  113 us
    pallas_call x1, Pallas kernels, per_device(): pl.pallas_call(copy_out, out_shape=tuple((jax.ShapeDtypeStruct(r.shape, r...  2.73 us

profile of v3, /device:TPU:4, one launch (start us, length us, event | category | flops | bytes accessed | tf_op | source)
XLA Modules:
  0.0 116.2 jit_solution(14417170953596313040)
XLA Ops:
  0.6 112.9 %swiglu.1 = (bf16[48,640]{1,0:T(8,128)(2,1)}, bf16[48,640]{1,0:T(8,128)(2,1)}, bf16[320,896]{1,0:T(8,128)(2,1)}, bf16[320,896]{1,0:T(8,128)(2,1)}, bf16[320,896]{1,0:T(8,128)(2,1)}) custom-call(bf16[48,640]{1,0:T(8,128)(2,1)} %tok.1, bf16[640,896]{1,0:T(8,128)(2,1)} %wg_h.1, bf16[640,896]{1,0:T(8,128)(2,1)} %wu_h.1, bf16[896,640]{1,0:T(8,128)(2,1)} %wd_h.1, ...), custom_call_target="tpu_custom_call" | custom-call | tf_op jit(solution)/shard_map/swiglu/pallas_call | solution.py:611
  113.5 2.7 %copy_out.1 = (bf16[48,640]{1,0:T(8,128)(2,1)}, bf16[48,640]{1,0:T(8,128)(2,1)}, bf16[320,896]{1,0:T(8,128)(2,1)}, bf16[320,896]{1,0:T(8,128)(2,1)}, bf16[320,896]{1,0:T(8,128)(2,1)}) custom-call(bf16[48,640]{1,0:T(8,128)(2,1)} %get-tuple-element.15.refs_0_, bf16[48,640]{1,0:T(8,128)(2,1)} %get-tuple-element.16.refs_1_, ...), custom_call_target="tpu_custom_call" | custom-call | tf_op jit(solution)/shard_map/copy_out/pallas_call | solution.py:628

commit v4 on v3

--- a/solution.py
+++ b/solution.py
@@ -494,11 +494,11 @@
     grads(pl.ds(CUT, width - CUT), y_first_sum(h2_f, h2_y, h2_x, h21, h22))
     hid1.relay2()
     hid0.relay3()
-    gr0.relay1()
     hid0.rest()
     dw0 = weight_grad(go_t, hid, 2 * width, 0, CUT, False)
     hid1.rest()
     dw1 = weight_grad(go_t, hid, 2 * width, CUT, width, False)
+    gr0.relay1()
     gr1.relay1()
     gr0.relay2()
     gr2 = XThenY(gr_a, CUT, 768)

time: 117 us -> 117 us (level)
  no operation moved by 1% of the time
where the time goes in v4:
time: 117 us; the launch traced here: 116 us
  Pallas kernels  116 us (99%)
    pallas_call x1, Pallas kernels, per_device(): pl.pallas_call(kernel, out_shape=(jax.ShapeDtypeStruct((n_tok, d), BF16),...  113 us
    pallas_call x1, Pallas kernels, per_device(): pl.pallas_call(copy_out, out_shape=tuple((jax.ShapeDtypeStruct(r.shape, r...  2.73 us

profile of v4, /device:TPU:4, one launch (start us, length us, event | category | flops | bytes accessed | tf_op | source)
XLA Modules:
  0.0 116.2 jit_solution(13446001713691418820)
XLA Ops:
  0.6 112.9 %swiglu.1 = (bf16[48,640]{1,0:T(8,128)(2,1)}, bf16[48,640]{1,0:T(8,128)(2,1)}, bf16[320,896]{1,0:T(8,128)(2,1)}, bf16[320,896]{1,0:T(8,128)(2,1)}, bf16[320,896]{1,0:T(8,128)(2,1)}) custom-call(bf16[48,640]{1,0:T(8,128)(2,1)} %tok.1, bf16[640,896]{1,0:T(8,128)(2,1)} %wg_h.1, bf16[640,896]{1,0:T(8,128)(2,1)} %wu_h.1, bf16[896,640]{1,0:T(8,128)(2,1)} %wd_h.1, ...), custom_call_target="tpu_custom_call" | custom-call | tf_op jit(solution)/shard_map/swiglu/pallas_call | solution.py:611
  113.5 2.7 %copy_out.1 = (bf16[48,640]{1,0:T(8,128)(2,1)}, bf16[48,640]{1,0:T(8,128)(2,1)}, bf16[320,896]{1,0:T(8,128)(2,1)}, bf16[320,896]{1,0:T(8,128)(2,1)}, bf16[320,896]{1,0:T(8,128)(2,1)}) custom-call(bf16[48,640]{1,0:T(8,128)(2,1)} %get-tuple-element.15.refs_0_, bf16[48,640]{1,0:T(8,128)(2,1)} %get-tuple-element.16.refs_1_, ...), custom_call_target="tpu_custom_call" | custom-call | tf_op jit(solution)/shard_map/copy_out/pallas_call | solution.py:628
